TPU v7x, 512 devices: a whole 4x4x16 slice. The times are simulated.
512 devices in a mesh: member: 16 (over y, z_hi), dp: 32 (over x, z_lo, core).
Axes of the slice: x: 4, y: 4, z: 16 (z_hi: 4, z_lo: 4; z = z_hi * 4 + z_lo), core: 2. Of those that a mesh axis runs over, the one named last changes fastest.
Arguments:
- features: bfloat16 [16, 512, 49, 1024], P('member', 'dp'), may hold values from -8 to 8
- labels: int32 [512], replicated, may hold values from 0 to 24575
- norm_gain: float32 [16, 1024], P('member'), may hold values from 0.75 to 1.25
- norm_bias: float32 [16, 1024], P('member'), may hold values from -0.25 to 0.25
- head_weight: bfloat16 [16, 1024, 24576], P('member', None, 'dp'), may hold values from -3 to 3
- head_bias: float32 [16, 24576], P('member', 'dp'), may hold values from -1.25 to 1.25
Outputs:
- mean_loss: float32 [], replicated
- grad_pooled: float32 [16, 512, 1024], P('member', 'dp')
- grad_gain: float32 [16, 1024], P('member')
- grad_bias: float32 [16, 1024], P('member')
- grad_head_weight: bfloat16 [16, 1024, 24576], P('member', None, 'dp')
- grad_head_bias: float32 [16, 24576], P('member', 'dp')
All inputs are finite; a program needn't handle non-finite values.
Results may differ from a plain program's by a relative error of at most 0.025.
Values may be sent and summed in bfloat16 or wider, within the bound.
No kernel may reach another device: no remote copies, remote signals or barrier semaphores. Data moves between devices by JAX's collectives and lax.ppermute only.
A program may use at most 64 MiB of HBM per device.

v0:
```python
import math
import jax
import jax.numpy as jnp
from jax import lax
from jax.sharding import PartitionSpec as P

norm_eps = 1e-06
loss_scale = 16.0


def merged(x, axis, combine):
    everything = jax.tree.map(lambda part: lax.all_gather(part, axis), x)
    initial = jax.tree.map(lambda part: part[0], everything)

    def hop(k, so_far):
        return combine(so_far, jax.tree.map(lambda part: part[k], everything))

    return lax.fori_loop(1, lax.axis_size(axis), hop, initial)


def layer_norm(pooled, norm_gain, norm_shift):
    center = pooled - jnp.mean(pooled, axis=-1, keepdims=True)
    inverse = lax.rsqrt(jnp.mean(center * center, axis=-1, keepdims=True) + norm_eps)
    normed = center * inverse
    return (normed, inverse, (normed * norm_gain + norm_shift).astype(jnp.bfloat16))


def norm_backward(upstream, normed, inverse, norm_gain):
    scaled = upstream * norm_gain
    return inverse * (
        scaled
        - jnp.mean(scaled, axis=-1, keepdims=True)
        - normed * jnp.mean(scaled * normed, axis=-1, keepdims=True)
    )


def member_join(former, latter):
    highest = jnp.maximum(former[0], latter[0])
    return (
        highest,
        former[1] * jnp.exp(former[0] - highest) + latter[1] * jnp.exp(latter[0] - highest),
    )


def per_device(features, labels, norm_gain, norm_bias, head_weight, head_bias):
    weight = head_weight[0]
    classes_here = weight.shape[1]
    gain_row = norm_gain[0]
    shift_row = norm_bias[0]
    position = lax.axis_index("dp")
    pooled = jnp.sum(features[0], axis=1, dtype=jnp.float32) / features.shape[2]
    normed, inverse, act = layer_norm(pooled, gain_row, shift_row)
    act_all = lax.all_gather(act, "dp", axis=0, tiled=True)
    logits = jnp.dot(act_all, weight, preferred_element_type=jnp.float32) + head_bias[0]
    local_class = labels - position * classes_here
    onehot = (local_class[:, None] == jnp.arange(classes_here, dtype=jnp.int32)[None, :]).astype(
        jnp.float32
    )
    label_part = jnp.sum(logits * onehot, axis=1)
    top_part = jnp.max(logits, axis=1)
    sum_part = jnp.sum(jnp.exp(logits - top_part[:, None]), axis=1)
    top_all = lax.pmax(top_part, "dp")
    sum_all, label_logit = lax.psum((sum_part * jnp.exp(top_part - top_all), label_part), "dp")
    log_total = top_all + jnp.log(sum_all)
    label_logp = label_logit - log_total
    mix_top, mix_sum = merged((label_logp, jnp.ones_like(label_logp)), "member", member_join)
    log_joint = mix_top + jnp.log(mix_sum)
    mean_loss = math.log(lax.axis_size("member")) - jnp.mean(log_joint)
    respons = jnp.exp(label_logp - log_joint)
    probabilities = jnp.exp(logits - log_total[:, None])
    grad_logits = (loss_scale * respons)[:, None] * (probabilities - onehot)
    grad_low = grad_logits.astype(jnp.bfloat16)
    grad_head_bias = jnp.sum(grad_logits, axis=0)
    grad_head_weight = lax.dot_general(
        act_all, grad_low, (((0,), (0,)), ((), ())), preferred_element_type=jnp.float32
    ).astype(jnp.bfloat16)
    upstream = lax.psum_scatter(
        lax.dot_general(
            grad_low, weight, (((1,), (1,)), ((), ())), preferred_element_type=jnp.float32
        ),
        "dp",
        scatter_dimension=0,
        tiled=True,
    )
    grad_gain, grad_shift = lax.psum(
        (jnp.sum(upstream * normed, axis=0), jnp.sum(upstream, axis=0)), "dp"
    )
    grad_pooled = norm_backward(upstream, normed, inverse, gain_row)
    return (
        mean_loss,
        grad_pooled[None],
        grad_gain[None],
        grad_shift[None],
        grad_head_weight[None],
        grad_head_bias[None],
    )


def solution(mesh):
    in_specs = (
        P("member", "dp", None, None),
        P(),
        P("member", None),
        P("member", None),
        P("member", None, "dp"),
        P("member", "dp"),
    )
    out_specs = (
        P(),
        P("member", "dp", None),
        P("member", None),
        P("member", None),
        P("member", None, "dp"),
        P("member", "dp"),
    )
    return jax.shard_map(
        per_device, mesh=mesh, in_specs=in_specs, out_specs=out_specs, check_vma=False
    )
```

profile of v0, /device:TPU:1, one launch (start us, length us, event | category | flops | bytes accessed | tf_op | source)
XLA Modules:
  0.0 497.9 jit_solution(16176686166835715571)
XLA Ops:
  7.2 0.0 copy-start
  7.2 0.0 copy-start.2
  7.2 0.0 copy-start.1
  7.2 0.0 copy-start.3
  7.2 0.0 copy-start.4
  7.2 0.0 all-gather.4.cloned.1.call-start
  7.3 1.8 convert_reduce_fusion
  9.0 0.1 multiply_reduce_fusion.4
  9.2 0.2 multiply_reduce_fusion.2
  9.4 0.0 copy-done.2
  9.4 0.0 copy-done.1
  9.4 0.7 add_convert_fusion
  10.1 0.0 all-gather.4.cloned.1.call-update
  10.1 0.0 reduce-scatter.2.cloned.1.call-start
  10.2 0.0 copy-done.3
  10.2 0.0 copy-done.4
  10.2 70.3 %all-gather.4.cloned.1.call-done = bf16[512,1024]{1,0:T(8,128)(2,1)} async-done(((bf16[16,1024]{1,0:T(8,128)(2,1)}), bf16[512,1024]{1,0:T(8,128)(2,1)}) %all-gather.4.cloned.1.call-update) | async-done | bytes 1048592 | tf_op jit(solution)/shard_map/all_gather | solution.py:53
  80.5 0.0 copy-done
  80.5 2.3 fusion.15
  82.8 67.0 %pmax.7 = f32[512]{0:T(512)S(1)} all-reduce(f32[512]{0:T(512)S(1)} %get-tuple-element.169), channel_id=1, replica_groups=mesh['member'=16,'dp'=32] {'dp'}, use_global_device_ids=true, to_apply=%region_6.0 | all-reduce | flops 512 | bytes 4096 | tf_op jit(solution)/shard_map/pmax | solution.py:62
  149.8 0.6 exponential_reduce_fusion
  150.4 70.2 %all-reduce.1 = (f32[512]{0:T(512)S(1)}, f32[512]{0:T(512)S(1)}) all-reduce(f32[512]{0:T(512)S(1)} %get-tuple-element.146, f32[512]{0:T(512)S(1)} %exponential_multiply_fusion.1), channel_id=1, replica_groups=mesh['member'=16,'dp'=32] {'dp'}, use_global_device_ids=true, to_apply=%region_4.0 | all-reduce | flops 1024 | bytes 8192 | tf_op jit(solution)/shard_map/psum | solution.py:63
  220.6 45.5 %all-gather.1 = f32[16,1,512]{2,1,0:T(1,128)S(1)} all-gather(f32[1,1,512]{2,1,0:T(1,128)S(1)} %bitcast.33), channel_id=2, replica_groups=mesh['member'=16,'dp'=32] {'member'}, dimensions={0}, use_global_device_ids=true | all-gather | bytes 34816 | tf_op jit(solution)/shard_map/all_gather | solution.py:12
  266.1 0.9 while.18
  267.0 0.6 exponential_multiply_fusion
  267.6 2.5 fusion.1
  270.1 0.0 reduce-scatter.2.cloned.1.call-update
  270.2 0.5 fusion.9
  270.7 0.6 broadcast_in_dim.28
  271.9 3.7 fusion.8
  275.6 138.1 %reduce-scatter.2.cloned.1.call-done = f32[16,1024]{1,0:T(8,128)} async-done(((f32[512,1024]{1,0:T(8,128)}), f32[16,1024]{1,0:T(8,128)}) %reduce-scatter.2.cloned.1.call-update) | async-done | bytes 65552 | tf_op jit(solution)/shard_map/reduce_scatter | solution.py:77
  413.7 1.0 multiply_reduce_fusion
  414.8 73.6 %all-reduce = (f32[1,1024]{1,0:T(1,128)}, f32[1,1024]{1,0:T(1,128)}) all-reduce(f32[1,1024]{1,0:T(1,128)S(1)} %bitcast.34, f32[1,1024]{1,0:T(1,128)S(1)} %bitcast.35), channel_id=1, replica_groups=mesh['member'=16,'dp'=32] {'dp'}, use_global_device_ids=true, to_apply=%region_16.0 | all-reduce | flops 2048 | bytes 16384 | tf_op jit(solution)/shard_map/psum | solution.py:85
  488.4 1.6 multiply_bitcast_fusion
  (40 shorter events, 0.5 us)
Async XLA Ops:
  7.2 73.4 %copy-start = (bf16[1,1024,768]{2,1,0:T(8,128)(2,1)S(1)}, bf16[1,1024,768]{2,1,0:T(8,128)(2,1)}, u32[]{:S(2)}) copy-start(bf16[1,1024,768]{2,1,0:T(8,128)(2,1)} %param.12) | copy-start | bytes 4718596
  7.2 2.2 copy-start.2
  7.2 2.2 copy-start.1
  7.2 3.0 copy-start.3
  7.2 3.0 copy-start.4
  7.2 73.3 %all-gather.4.cloned.1.call-start = ((), (), s32[]{:S(2)}) async-start(), calls=%async_computation.1 | async-start | bytes 1081344 | tf_op jit(solution)/shard_map/all_gather | solution.py:53
  10.1 403.6 %reduce-scatter.2.cloned.1.call-start = ((), (), s32[]{:S(2)}) async-start(), calls=%async_computation.2 | async-start | bytes 2162688 | tf_op jit(solution)/shard_map/reduce_scatter | solution.py:77
Sparse Core Ops, SparseCore 0:
  10.8 69.6 all-gather.3
  270.3 143.3 reduce-scatter.1
where the time goes:
time: 498 us
  blocking collectives  256 us (51%)
  waiting for transfers between devices  208 us (42%)
  between operations  16 us (3%)
  matrix products  8.5 us (2%)
  other arithmetic  7.42 us (1%)
    reduce_scatter x1, waiting for transfers between devices, per_device(): lax.psum_scatter(lax.dot_general(grad_low, weight, (((1,), (1,)), ((), ()...  138 us
    psum x1, blocking collectives, per_device(): lax.psum((jnp.sum(upstream * normed, axis=0), jnp.sum(upstream, axis=0)),...  73.6 us
    all_gather x1, waiting for transfers between devices, per_device(): act_all = lax.all_gather(act, 'dp', axis=0, tiled=True)  70.3 us
    psum x1, blocking collectives, per_device(): lax.psum((sum_part * jnp.exp(top_part - top_all), label_part), 'dp')  70.2 us
    pmax x1, blocking collectives, per_device(): top_all = lax.pmax(top_part, 'dp')  67 us
    all_gather x1, blocking collectives, merged(): everything = jax.tree.map(lambda part: lax.all_gather(part, axis), x)  45.5 us
  transfers between devices with their start and end apart: 2, of which 2 were waited for; matrix products, arithmetic and copies ran while one was open for 1% of the time, Pallas kernels for 0%

commit v1 on v0

--- a/solution.py
+++ b/solution.py
@@ -50,7 +50,15 @@
     position = lax.axis_index("dp")
     pooled = jnp.sum(features[0], axis=1, dtype=jnp.float32) / features.shape[2]
     normed, inverse, act = layer_norm(pooled, gain_row, shift_row)
-    act_all = lax.all_gather(act, "dp", axis=0, tiled=True)
+
+    def unite_seats_all(where_dim, which_axis, tile_in):
+        piece_out = lax.psum(1, axis_name=which_axis)
+        reply = lax.all_to_all(
+            jnp.stack([tile_in] * piece_out), concat_axis=0, split_axis=0, axis_name=which_axis
+        )
+        return jnp.concatenate(reply, axis=where_dim)
+
+    act_all = unite_seats_all(0, "dp", act)
     logits = jnp.dot(act_all, weight, preferred_element_type=jnp.float32) + head_bias[0]
     local_class = labels - position * classes_here
     onehot = (local_class[:, None] == jnp.arange(classes_here, dtype=jnp.int32)[None, :]).astype(

time: 498 us -> 470 us (0.944)
  waiting for transfers between devices: 208 us -> 166 us
  starting transfers between devices: 0.08 us -> 10.5 us
    all_gather x1 -> x0, waiting for transfers between devices: 70.3 us -> none  [per_device(): act_all = lax.all_gather(act, 'dp', axis=0, tiled=True)]
    all_to_all x0 -> x1, waiting for transfers between devices: none -> 27.9 us  [unite_seats_all(): lax.all_to_all(jnp.stack([tile_in] * piece_out), concat_axis=0, split_axi...]
    all_to_all x0 -> x1, starting transfers between devices: none -> 10.5 us  [unite_seats_all(): lax.all_to_all(jnp.stack([tile_in] * piece_out), concat_axis=0, split_axi...]
where the time goes in v1:
time: 470 us; the launch traced here: 469 us
  blocking collectives  258 us (55%)
  waiting for transfers between devices  166 us (35%)
  between operations  16 us (3%)
  starting transfers between devices  10.5 us (2%)
  matrix products  8.51 us (2%)
  other arithmetic  6.82 us (1%)
    reduce_scatter x1, waiting for transfers between devices, per_device(): lax.psum_scatter(lax.dot_general(grad_low, weight, (((1,), (1,)), ((), ()...  138 us
    psum x1, blocking collectives, per_device(): lax.psum((jnp.sum(upstream * normed, axis=0), jnp.sum(upstream, axis=0)),...  74 us
    psum x1, blocking collectives, per_device(): lax.psum((sum_part * jnp.exp(top_part - top_all), label_part), 'dp')  68.8 us
    pmax x1, blocking collectives, per_device(): top_all = lax.pmax(top_part, 'dp')  67 us
    all_gather x1, blocking collectives, merged(): everything = jax.tree.map(lambda part: lax.all_gather(part, axis), x)  48.2 us
    all_to_all x1, waiting for transfers between devices, unite_seats_all(): lax.all_to_all(jnp.stack([tile_in] * piece_out), concat_axis=0, split_axi...  27.9 us
    all_to_all x1, starting transfers between devices, unite_seats_all(): lax.all_to_all(jnp.stack([tile_in] * piece_out), concat_axis=0, split_axi...  10.5 us
  transfers between devices with their start and end apart: 2, of which 2 were waited for; matrix products, arithmetic and copies ran while one was open for 1% of the time, Pallas kernels for 0%

profile of v1, /device:TPU:1, one launch (start us, length us, event | category | flops | bytes accessed | tf_op | source)
XLA Modules:
  0.0 469.5 jit_solution(12146186090499567146)
XLA Ops:
  7.2 0.0 copy-start
  7.2 0.0 copy-start.3
  7.2 0.0 copy-start.2
  7.2 1.8 convert_reduce_fusion
  9.0 0.1 multiply_reduce_fusion.4
  9.1 0.2 multiply_reduce_fusion.2
  9.3 0.0 copy-done.3
  9.3 0.0 copy-done.2
  9.3 0.1 add_convert_fusion
  9.4 0.0 copy-start.4
  9.4 0.0 copy-start.5
  9.4 1.1 stack.2
  10.5 10.5 %all-to-all-start = ((bf16[32,16,1024]{2,1,0:T(8,128)(2,1)}), bf16[32,16,1024]{2,1,0:T(8,128)(2,1)S(1)}, u32[]{:S(2)}, u32[]{:S(2)}) async-start(bf16[32,16,1024]{2,1,0:T(8,128)(2,1)} %stack.2), calls=%async_computation | async-start | bytes 2097152 | tf_op jit(solution)/shard_map/all_to_all | solution.py:56
  21.0 0.0 reduce-scatter.2.cloned.1.call-start
  21.1 0.0 copy-done.4
  21.1 0.0 copy-done.5
  21.1 27.9 %all-to-all-done = bf16[32,16,1024]{2,1,0:T(8,128)(2,1)S(1)} async-done(((bf16[32,16,1024]{2,1,0:T(8,128)(2,1)}), bf16[32,16,1024]{2,1,0:T(8,128)(2,1)S(1)}, u32[]{:S(2)}, u32[]{:S(2)}) %all-to-all-start) | async-done | bytes 1048608 | tf_op jit(solution)/shard_map/all_to_all | solution.py:56
  49.0 0.0 copy-start.1
  49.0 1.0 copy-done.1
  50.0 0.0 copy-done
  50.0 2.3 fusion.15
  52.3 67.0 %pmax.7 = f32[512]{0:T(512)S(1)} all-reduce(f32[512]{0:T(512)S(1)} %get-tuple-element.169), channel_id=1, replica_groups=mesh['member'=16,'dp'=32] {'dp'}, use_global_device_ids=true, to_apply=%region_6.0 | all-reduce | flops 512 | bytes 4096 | tf_op jit(solution)/shard_map/pmax | solution.py:70
  119.3 0.6 exponential_reduce_fusion
  119.9 68.8 %all-reduce.1 = (f32[512]{0:T(512)S(1)}, f32[512]{0:T(512)S(1)}) all-reduce(f32[512]{0:T(512)S(1)} %get-tuple-element.146, f32[512]{0:T(512)S(1)} %exponential_multiply_fusion.1), channel_id=1, replica_groups=mesh['member'=16,'dp'=32] {'dp'}, use_global_device_ids=true, to_apply=%region_4.0 | all-reduce | flops 1024 | bytes 8192 | tf_op jit(solution)/shard_map/psum | solution.py:71
  188.7 48.2 %all-gather.1 = f32[16,1,512]{2,1,0:T(1,128)S(1)} all-gather(f32[1,1,512]{2,1,0:T(1,128)S(1)} %bitcast.36), channel_id=2, replica_groups=mesh['member'=16,'dp'=32] {'member'}, dimensions={0}, use_global_device_ids=true | all-gather | bytes 34816 | tf_op jit(solution)/shard_map/all_gather | solution.py:12
  236.9 0.9 while.18
  237.8 0.6 exponential_multiply_fusion
  238.5 2.6 fusion.1
  241.0 0.0 reduce-scatter.2.cloned.1.call-update
  241.0 0.5 fusion.9
  241.6 0.6 broadcast_in_dim.28
  242.8 3.7 fusion.8
  246.5 138.4 %reduce-scatter.2.cloned.1.call-done = f32[16,1024]{1,0:T(8,128)} async-done(((f32[512,1024]{1,0:T(8,128)}), f32[16,1024]{1,0:T(8,128)}) %reduce-scatter.2.cloned.1.call-update) | async-done | bytes 65552 | tf_op jit(solution)/shard_map/reduce_scatter | solution.py:85
  384.9 1.0 multiply_reduce_fusion
  386.0 74.0 %all-reduce = (f32[1,1024]{1,0:T(1,128)}, f32[1,1024]{1,0:T(1,128)}) all-reduce(f32[1,1024]{1,0:T(1,128)S(1)} %bitcast.37, f32[1,1024]{1,0:T(1,128)S(1)} %bitcast.38), channel_id=1, replica_groups=mesh['member'=16,'dp'=32] {'dp'}, use_global_device_ids=true, to_apply=%region_16.0 | all-reduce | flops 2048 | bytes 16384 | tf_op jit(solution)/shard_map/psum | solution.py:93
  460.0 1.6 multiply_bitcast_fusion
  (40 shorter events, 0.5 us)
Async XLA Ops:
  7.2 42.8 %copy-start = (bf16[1,1024,768]{2,1,0:T(8,128)(2,1)S(1)}, bf16[1,1024,768]{2,1,0:T(8,128)(2,1)}, u32[]{:S(2)}) copy-start(bf16[1,1024,768]{2,1,0:T(8,128)(2,1)} %param.12) | copy-start | bytes 4718596
  7.2 2.1 copy-start.3
  7.2 2.1 copy-start.2
  9.4 11.7 %copy-start.4 = (f32[1,768]{1,0:T(1,128)S(1)}, f32[1,768]{1,0:T(1,128)}, u32[]{:S(2)}) copy-start(f32[1,768]{1,0:T(1,128)} %param.13) | copy-start | bytes 9220
  9.4 11.7 %copy-start.5 = (s32[512]{0:T(512)S(1)}, s32[512]{0:T(512)}, u32[]{:S(2)}) copy-start(s32[512]{0:T(512)} %param.9) | copy-start | bytes 6148
  10.5 38.5 %all-to-all-start = ((bf16[32,16,1024]{2,1,0:T(8,128)(2,1)}), bf16[32,16,1024]{2,1,0:T(8,128)(2,1)S(1)}, u32[]{:S(2)}, u32[]{:S(2)}) async-start(bf16[32,16,1024]{2,1,0:T(8,128)(2,1)} %stack.2), calls=%async_computation | async-start | bytes 2097152 | tf_op jit(solution)/shard_map/all_to_all | solution.py:56
  21.0 363.9 %reduce-scatter.2.cloned.1.call-start = ((), (), s32[]{:S(2)}) async-start(), calls=%async_computation.2 | async-start | bytes 2162688 | tf_op jit(solution)/shard_map/reduce_scatter | solution.py:85
  49.0 1.0 copy-start.1
Sparse Core Ops, SparseCore 0:
  241.2 143.6 reduce-scatter.1
